TPU v7x, 256 devices: a whole 4x4x8 slice. The times are simulated.
256 devices in a mesh: row: 32 (over x, z), feat: 8 (over y, core).
Axes of the slice: x: 4, y: 4, z: 8, core: 2. Of those that a mesh axis runs over, the one named last changes fastest.
Arguments:
- candidates: bfloat16 [2048, 16384], P('row', 'feat'), may hold values from -48 to 48, as said below
- inv_factor: bfloat16 [16384, 16384], P('row', 'feat'), may hold values from -1.5 to 1.5, as said below
- weights: float32 [2048], P('row'), may hold values from 0.01 to 0.1
- strata: int32 [2048], P('row'), may hold values from 0 to 63, never falling along the last dimension, each value on 1 to 256 neighbouring positions
Outputs:
- new_weight: float32 [2048], P('row')
- leverage: float32 [2048], P('row')
- information: float32 [16384, 16384], P('row', 'feat')
Inputs may be any that keep to these rules, and one draw needn't show every extreme that they name: `candidates`: row scales and column scales differ. `inv_factor`: zero above the diagonal, positive on the diagonal.
All inputs are finite; a program needn't handle non-finite values.
Results may differ from a plain program's by a relative error of at most 0.0029.
Values may be sent and summed in bfloat16 or wider, within the bound.
A program may use at most 64 MiB of HBM per device.

v0:
```python
import jax
import jax.numpy as jnp
from jax import lax
from jax.sharding import PartitionSpec as P


def broadcast(shard, axis, root):
    mine = lax.axis_index(axis) == root
    return lax.psum(jnp.where(mine, shard, jnp.zeros_like(shard)), axis)


def per_device(candidates, inv_factor, weights, strata):
    rows_dev = candidates.shape[0]
    feat_block = candidates.shape[1]
    row_block = inv_factor.shape[0]
    row_count = lax.axis_size("row")
    feat_count = lax.axis_size("feat")
    features = feat_block * feat_count
    gathered = lax.all_gather(candidates, "row", axis=0, tiled=True)
    partial_value = lax.dot_general(
        gathered, inv_factor, (((1,), (1,)), ((), ())), preferred_element_type=jnp.float32
    )
    shaped = partial_value.reshape(row_count, rows_dev, row_block)
    summed = lax.psum_scatter(shaped, "feat", scatter_dimension=1, tiled=True)
    squares = jnp.sum(summed * summed, axis=2)
    reduced = lax.psum_scatter(squares, "row", scatter_dimension=0, tiled=True)
    raw_leverage = lax.all_gather(reduced, "feat", axis=1, tiled=True).reshape(rows_dev)
    leverage = raw_leverage / features
    strata_count = 2 * row_count
    membership = (strata[:, None] == jnp.arange(strata_count, dtype=jnp.int32)[None, :]).astype(
        jnp.float32
    )
    products = weights * raw_leverage
    local_product = lax.dot_general(
        membership, products, (((0,), (0,)), ((), ())), precision=lax.Precision.HIGHEST
    )
    local_mass = lax.dot_general(
        membership, weights, (((0,), (0,)), ((), ())), precision=lax.Precision.HIGHEST
    )
    stratum_product, stratum_mass = lax.psum((local_product, local_mass), "row")
    stratum_ratio = stratum_mass / stratum_product
    row_ratio = jnp.dot(membership, stratum_ratio, precision=lax.Precision.HIGHEST)
    new_weight = products * row_ratio
    weight_step = new_weight - weights
    step_all = lax.all_gather(weight_step, "row", axis=0, tiled=True)
    scaled_all = (step_all[:, None] * gathered.astype(jnp.float32)).astype(jnp.bfloat16)
    blocks_per_feat = row_count // feat_count
    row_index = lax.axis_index("row")
    offset = row_index % blocks_per_feat * row_block
    mine = lax.dynamic_slice_in_dim(gathered, offset, row_block, 1)
    root_index = row_index // blocks_per_feat
    column_block = broadcast(mine, "feat", root_index)
    information = lax.dot_general(
        column_block, scaled_all, (((0,), (0,)), ((), ())), preferred_element_type=jnp.float32
    )
    return (new_weight, leverage, information)


def solution(mesh):
    in_specs = (P("row", "feat"), P("row", "feat"), P("row"), P("row"))
    out_specs = (P("row"), P("row"), P("row", "feat"))
    return jax.shard_map(
        per_device, mesh=mesh, in_specs=in_specs, out_specs=out_specs, check_vma=False
    )
```

profile of v0, /device:TPU:0, one launch (start us, length us, event | category | flops | bytes accessed | tf_op | source)
XLA Modules:
  0.0 475.3 jit_solution(4714383224408392123)
XLA Ops:
  7.2 0.0 copy-start
  7.2 0.0 all-gather.2.cloned.1.call-start
  7.2 0.7 all-gather.2.cloned.1.call-update
  7.9 0.0 reduce-scatter.2.cloned.1.call-start
  8.0 102.2 %all-gather.2.cloned.1.call-done = bf16[2048,2048]{1,0:T(8,128)(2,1)} async-done(((bf16[64,2048]{1,0:T(8,128)(2,1)}), bf16[2048,2048]{1,0:T(8,128)(2,1)}) %all-gather.2.cloned.1.call-update) | async-done | bytes 8388624 | tf_op jit(solution)/shard_map/all_gather | solution.py:19
  110.2 0.0 copy-done
  110.2 9.5 %fusion.12 = f32[2048,512]{1,0:T(8,128)} fusion(bf16[2048,2048]{1,0:T(8,128)(2,1)} %all-gather.2.cloned.1.call-done, bf16[512,2048]{1,0:T(8,128)(2,1)S(1)} %copy-done), kind=kOutput, calls=%fused_computation.22 | convolution fusion | flops 4294967296 | bytes 14680064 | tf_op jit(solution)/shard_map/dot_general | solution.py:20
  119.7 0.0 reduce-scatter.2.cloned.1.call-update
  119.7 0.0 copy-start.1
  119.7 0.0 copy-start.4
  119.7 0.0 copy-start.5
  119.7 0.0 copy-start.2
  119.7 0.0 all-reduce.6.cloned.1.call-start
  119.8 3.3 dynamic-slice_select_fusion
  123.1 0.0 all-reduce.6.cloned.1.call-update
  123.1 0.2 convolution_bitcast_fusion.2
  123.3 0.6 dynamic-slice
  124.6 0.6 fusion.11
  125.9 31.5 %reduce-scatter.2.cloned.1.call-done = f32[32,8,512]{2,1,0:T(8,128)} async-done(((f32[32,64,512]{2,1,0:T(8,128)}), f32[32,8,512]{2,1,0:T(8,128)}) %reduce-scatter.2.cloned.1.call-update) | async-done | bytes 524304 | tf_op jit(solution)/shard_map/reduce_scatter | solution.py:24
  157.4 1.2 multiply_reduce_fusion
  158.5 143.1 %all-reduce.2 = f32[32,8]{1,0:T(8,128)S(1)} all-reduce(f32[32,8]{1,0:T(8,128)S(1)} %multiply_reduce_fusion), channel_id=3, replica_groups=mesh['row'=32,'feat'=8] {'row'}, use_global_device_ids=true, to_apply=%region_2.0.clone | all-reduce | flops 256 | bytes 2048
  301.6 0.7 fusion.6
  302.3 12.4 %all-reduce = f32[64]{0:T(128)S(1)} all-reduce(f32[64]{0:T(128)S(1)} %fusion.6), channel_id=1, replica_groups=mesh['row'=32,'feat'=8] {'feat'}, use_global_device_ids=true, to_apply=%add | all-reduce | flops 64 | bytes 512 | tf_op jit(solution)/shard_map/reshape | solution.py:27
  314.7 0.5 broadcast_multiply_fusion
  315.2 0.2 convolution_bitcast_fusion.1
  315.4 69.6 %all-reduce.3 = (f32[64]{0:T(128)S(1)}, f32[64]{0:T(128)S(1)}) all-reduce(f32[64]{0:T(128)S(1)} %convolution_bitcast_fusion.2, f32[64]{0:T(128)S(1)} %convolution_bitcast_fusion.1), channel_id=1, replica_groups=mesh['row'=32,'feat'=8] {'row'}, use_global_device_ids=true, to_apply=%region_3.0 | all-reduce | flops 128 | bytes 1024 | tf_op jit(solution)/shard_map/psum | solution.py:40
  385.0 0.2 fusion.2
  385.2 0.1 subtract_dynamic-update-slice_fusion
  385.4 72.6 %all-reduce.1 = f32[2048]{0:T(1024)S(1)} all-reduce(f32[2048]{0:T(1024)S(1)} %subtract_dynamic-update-slice_fusion), channel_id=1, replica_groups=mesh['row'=32,'feat'=8] {'row'}, use_global_device_ids=true, to_apply=%add.1 | all-reduce | flops 2048 | bytes 16384
  458.0 0.0 all-reduce.6.cloned.1.call-done
  458.0 10.8 %fusion = f32[512,2048]{1,0:T(8,128)} fusion(bf16[2048,512]{1,0:T(8,128)(2,1)} %all-reduce.6.cloned.1.call-done, bf16[2048,2048]{1,0:T(8,128)(2,1)} %all-gather.2.cloned.1.call-done, f32[2048]{0:T(1024)S(1)} %all-reduce.1), kind=kOutput, calls=%fused_computation.1 | convolution fusion | flops 4307550208 | bytes 14688256 | tf_op jit(solution)/shard_map/dot_general | solution.py:53
  468.8 0.0 copy-done.3
  (7 shorter events, 0.0 us)
Async XLA Ops:
  7.2 103.0 %copy-start = (bf16[512,2048]{1,0:T(8,128)(2,1)S(1)}, bf16[512,2048]{1,0:T(8,128)(2,1)}, u32[]{:S(2)}) copy-start(bf16[512,2048]{1,0:T(8,128)(2,1)} %param.5) | copy-start | bytes 6291460
  7.2 103.0 %all-gather.2.cloned.1.call-start = ((), (), s32[]{:S(2)}) async-start(), calls=%async_computation.1 | async-start | bytes 8650752 | tf_op jit(solution)/shard_map/all_gather | solution.py:19
  7.9 149.5 %reduce-scatter.2.cloned.1.call-start = ((), (), s32[]{:S(2)}) async-start(), calls=%async_computation.2 | async-start | bytes 4718592 | tf_op jit(solution)/shard_map/reduce_scatter | solution.py:24
  119.7 3.4 copy-start.1
  119.7 3.4 copy-start.4
  119.7 3.6 copy-start.5
  119.7 4.8 %copy-start.2 = (u32[256]{0:T(256)S(1)}, u32[256]{0:T(256)}, u32[]{:S(2)}) copy-start(u32[256]{0:T(256)} %constant.54) | copy-start | bytes 3076
  119.7 338.3 %all-reduce.6.cloned.1.call-start = ((), (), s32[]{:S(2)}) async-start(), calls=%async_computation.3 | async-start | bytes 4194304 | tf_op jit(solution)/shard_map/psum | solution.py:9
  385.2 83.6 %copy-start.3 = (f32[64]{0:T(128)}, f32[64]{0:T(128)S(1)}, u32[]{:S(2)}) copy-start(f32[64]{0:T(128)S(1)} %fusion.2) | copy-start | bytes 772
Sparse Core Ops, SparseCore 0:
  10.6 99.5 all-gather.1
  119.8 37.5 reduce-scatter.1
  159.7 69.6 all-reduce.5
where the time goes:
time: 476 us; the launch traced here: 475 us
  blocking collectives  298 us (63%)
  waiting for transfers between devices  134 us (28%)
  matrix products  20.8 us (4%)
  between operations  15.2 us (3%)
  other arithmetic  5.06 us (1%)
    unnamed x2, blocking collectives  216 us
    all_gather x1, waiting for transfers between devices, per_device(): gathered = lax.all_gather(candidates, 'row', axis=0, tiled=True)  102 us
    psum x1, blocking collectives, per_device(): stratum_product, stratum_mass = lax.psum((local_product, local_mass), 'row')  69.6 us
    reduce_scatter x1, waiting for transfers between devices, per_device(): summed = lax.psum_scatter(shaped, 'feat', scatter_dimension=1, tiled=True)  31.5 us
    reshape x1, blocking collectives, per_device(): lax.all_gather(reduced, 'feat', axis=1, tiled=True).reshape(rows_dev)  12.4 us
    dot_general x1, matrix products, per_device(): lax.dot_general(column_block, scaled_all, (((0,), (0,)), ((), ())), prefe...  10.8 us
  transfers between devices with their start and end apart: 3, of which 2 were waited for; matrix products, arithmetic and copies ran while one was open for 2% of the time, Pallas kernels for 0%

commit v1 on v0

--- a/solution.py
+++ b/solution.py
@@ -16,7 +16,9 @@
     row_count = lax.axis_size("row")
     feat_count = lax.axis_size("feat")
     features = feat_block * feat_count
-    gathered = lax.all_gather(candidates, "row", axis=0, tiled=True)
+    gathered = jnp.concatenate(
+        lax.all_to_all(jnp.stack([candidates] * lax.axis_size("row")), "row", 0, 0), axis=0
+    )
     partial_value = lax.dot_general(
         gathered, inv_factor, (((1,), (1,)), ((), ())), preferred_element_type=jnp.float32
     )

time: 476 us -> 570 us (1.20)
  blocking collectives: 298 us -> 493 us
  waiting for transfers between devices: 134 us -> 31.2 us
    all_to_all x0 -> x1, blocking collectives: none -> 195 us  [per_device(): lax.all_to_all(jnp.stack([candidates] * lax.axis_size('row')), 'row', 0, 0)]
    all_gather x1 -> x0, waiting for transfers between devices: 102 us -> none  [per_device(): gathered = lax.all_gather(candidates, 'row', axis=0, tiled=True)]
  transfers between devices with their start and end apart: 3 -> 2, of which waited for: 2 -> 1; matrix products, arithmetic and copies ran while one was open for 2% -> 1% of each run, Pallas kernels for 0% -> 0%
where the time goes in v1:
time: 570 us
  blocking collectives  493 us (86%)
  waiting for transfers between devices  31.2 us (5%)
  matrix products  17.5 us (3%)
  between operations  15.5 us (3%)
  local copies, waits for them, and re-layouts  7.34 us (1%)
    unnamed x2, blocking collectives  216 us
    all_to_all x1, blocking collectives, per_device(): lax.all_to_all(jnp.stack([candidates] * lax.axis_size('row')), 'row', 0, 0)  195 us
    psum x1, blocking collectives, per_device(): stratum_product, stratum_mass = lax.psum((local_product, local_mass), 'row')  69.6 us
    reduce_scatter x1, waiting for transfers between devices, per_device(): summed = lax.psum_scatter(shaped, 'feat', scatter_dimension=1, tiled=True)  31.2 us
    reshape x1, blocking collectives, per_device(): lax.all_gather(reduced, 'feat', axis=1, tiled=True).reshape(rows_dev)  12.4 us
  transfers between devices with their start and end apart: 2, of which 1 were waited for; matrix products, arithmetic and copies ran while one was open for 1% of the time, Pallas kernels for 0%

profile of v1, /device:TPU:0, one launch (start us, length us, event | category | flops | bytes accessed | tf_op | source)
XLA Modules:
  0.0 569.6 jit_solution(10725776341283185809)
XLA Ops:
  7.2 0.0 copy-start
  7.2 0.0 reduce-scatter.2.cloned.1.call-start
  7.2 2.1 stack.2
  9.4 195.3 %all_to_all.5 = bf16[32,64,2048]{2,1,0:T(8,128)(2,1)S(1)} all-to-all(bf16[32,64,2048]{2,1,0:T(8,128)(2,1)S(1)} %stack.2), channel_id=1, replica_groups=mesh['row'=32,'feat'=8] {'row'}, dimensions={0} | all-to-all | bytes 16777216 | tf_op jit(solution)/shard_map/all_to_all | solution.py:20
  204.7 3.2 copy-done.1
  207.9 6.1 %fusion.2 = f32[32,64,512]{2,1,0:T(8,128)} fusion(bf16[32,64,2048]{2,1,0:T(8,128)(2,1)S(1)} %all_to_all.5, bf16[512,2048]{1,0:T(8,128)(2,1)S(1)} %copy-done), kind=kOutput, calls=%fused_computation.3 | convolution fusion | flops 4294967296 | bytes 14680064 | tf_op jit(solution)/shard_map/dot_general | solution.py:22
  214.0 0.0 reduce-scatter.2.cloned.1.call-update
  214.1 0.0 copy-start.2
  214.1 0.0 copy-start.5
  214.1 0.0 copy-start.6
  214.1 0.0 copy-start.3
  214.1 0.0 all-reduce.6.cloned.1.call-start
  214.2 3.3 dynamic-slice_select_fusion
  217.4 0.0 all-reduce.6.cloned.1.call-update
  217.5 0.0 copy-done.2
  217.5 0.0 copy-done.5
  217.5 0.2 convolution_bitcast_fusion.2
  217.7 0.6 dynamic-slice
  218.9 0.6 fusion.13
  220.2 31.2 %reduce-scatter.2.cloned.1.call-done = f32[32,8,512]{2,1,0:T(8,128)} async-done(((f32[32,64,512]{2,1,0:T(8,128)}), f32[32,8,512]{2,1,0:T(8,128)}) %reduce-scatter.2.cloned.1.call-update) | async-done | bytes 524304 | tf_op jit(solution)/shard_map/reduce_scatter | solution.py:26
  251.4 1.2 multiply_reduce_fusion
  252.5 143.0 %all-reduce.2 = f32[32,8]{1,0:T(8,128)S(1)} all-reduce(f32[32,8]{1,0:T(8,128)S(1)} %multiply_reduce_fusion), channel_id=3, replica_groups=mesh['row'=32,'feat'=8] {'row'}, use_global_device_ids=true, to_apply=%region_2.0.clone | all-reduce | flops 256 | bytes 2048
  395.6 0.7 fusion.8
  396.3 12.4 %all-reduce = f32[64]{0:T(128)S(1)} all-reduce(f32[64]{0:T(128)S(1)} %fusion.8), channel_id=1, replica_groups=mesh['row'=32,'feat'=8] {'feat'}, use_global_device_ids=true, to_apply=%add | all-reduce | flops 64 | bytes 512 | tf_op jit(solution)/shard_map/reshape | solution.py:29
  408.7 0.5 broadcast_multiply_fusion
  409.2 0.2 convolution_bitcast_fusion.1
  409.4 69.6 %all-reduce.3 = (f32[64]{0:T(128)S(1)}, f32[64]{0:T(128)S(1)}) all-reduce(f32[64]{0:T(128)S(1)} %convolution_bitcast_fusion.2, f32[64]{0:T(128)S(1)} %convolution_bitcast_fusion.1), channel_id=1, replica_groups=mesh['row'=32,'feat'=8] {'row'}, use_global_device_ids=true, to_apply=%region_3.0 | all-reduce | flops 128 | bytes 1024 | tf_op jit(solution)/shard_map/psum | solution.py:42
  479.0 0.2 fusion.4
  479.2 0.1 subtract_dynamic-update-slice_fusion
  479.3 72.6 %all-reduce.1 = f32[2048]{0:T(1024)S(1)} all-reduce(f32[2048]{0:T(1024)S(1)} %subtract_dynamic-update-slice_fusion), channel_id=1, replica_groups=mesh['row'=32,'feat'=8] {'row'}, use_global_device_ids=true, to_apply=%add.1 | all-reduce | flops 2048 | bytes 16384
  552.0 0.0 all-reduce.6.cloned.1.call-done
  552.0 10.8 %fusion = f32[512,2048]{1,0:T(8,128)} fusion(bf16[2048,512]{1,0:T(8,128)(2,1)} %all-reduce.6.cloned.1.call-done, bf16[2048,2048]{1,0:T(8,128)(2,1)} %bitcast.31, f32[2048]{0:T(1024)S(1)} %all-reduce.1), kind=kOutput, calls=%fused_computation.1 | convolution fusion | flops 4307550208 | bytes 14688256 | tf_op jit(solution)/shard_map/dot_general | solution.py:55
  (8 shorter events, 0.0 us)
Async XLA Ops:
  7.2 200.8 %copy-start = (bf16[512,2048]{1,0:T(8,128)(2,1)S(1)}, bf16[512,2048]{1,0:T(8,128)(2,1)}, u32[]{:S(2)}) copy-start(bf16[512,2048]{1,0:T(8,128)(2,1)} %param.5) | copy-start | bytes 6291460
  7.2 244.2 %reduce-scatter.2.cloned.1.call-start = ((), (), s32[]{:S(2)}) async-start(), calls=%async_computation.2 | async-start | bytes 4718592 | tf_op jit(solution)/shard_map/reduce_scatter | solution.py:26
  204.7 3.2 copy-start.1
  214.1 3.4 copy-start.2
  214.1 3.4 copy-start.5
  214.1 3.6 copy-start.6
  214.1 4.8 copy-start.3
  214.1 337.9 %all-reduce.6.cloned.1.call-start = ((), (), s32[]{:S(2)}) async-start(), calls=%async_computation.3 | async-start | bytes 4194304 | tf_op jit(solution)/shard_map/psum | solution.py:9
  479.2 83.6 %copy-start.4 = (f32[64]{0:T(128)}, f32[64]{0:T(128)S(1)}, u32[]{:S(2)}) copy-start(f32[64]{0:T(128)S(1)} %fusion.4) | copy-start | bytes 772
Sparse Core Ops, SparseCore 0:
  214.2 37.1 reduce-scatter.1
  253.7 69.9 all-reduce.5
